TPU v7x, 32 devices: a whole 2x2x4 slice. The times are simulated.
32 devices in a mesh: blk: 4 (over y, x), grp: 8 (over z, core).
Axes of the slice: x: 2, y: 2, z: 4, core: 2. Of those that a mesh axis runs over, the one named last changes fastest.
Arguments:
- image_embeds: bfloat16 [512, 1152], P(('blk', 'grp')), may hold values from -6 to 6
- text_embeds: bfloat16 [512, 1152], P(('blk', 'grp')), may hold values from -6 to 6
Outputs:
- image_grads: float32 [512, 1152], P(('blk', 'grp'))
- text_grads: float32 [512, 1152], P(('blk', 'grp'))
All inputs are finite; a program needn't handle non-finite values.
Results may differ from a plain program's by a relative error of at most 0.011.
Values may be sent and summed in bfloat16 or wider, within the bound.
A program may use at most 64 MiB of HBM per device.

v0:
```python
import jax
import jax.numpy as jnp
from jax import lax
from jax.sharding import PartitionSpec as P

LOGIT_SCALE = 0.044
LOGIT_BIAS = -4.0


def shifted(array, axis, by):
    peers = lax.axis_size(axis)
    return lax.ppermute(array, axis, [(i, (i + by) % peers) for i in range(peers)])


def local(image_embeds, text_embeds):
    row_count, feat_width = text_embeds.shape
    group_size = lax.axis_size("grp")
    cycle_length = lax.axis_size("blk")
    gathered = lax.all_gather(image_embeds, "grp", axis=0, tiled=True)
    group_rows = gathered.shape[0]
    block_index = lax.axis_index("blk")
    member_index = lax.axis_index("grp")
    image_ids = block_index * group_rows + jnp.arange(group_rows, dtype=jnp.int32)
    row_offsets = jnp.arange(row_count, dtype=jnp.int32)

    def compute_weights(visiting, anchor):
        logits = (
            LOGIT_SCALE
            * lax.dot_general(
                visiting, gathered, (((1,), (1,)), ((), ())), preferred_element_type=jnp.float32
            )
            + LOGIT_BIAS
        )
        text_ids = (anchor * group_size + member_index) * row_count + row_offsets
        labels = (text_ids[:, None] == image_ids[None, :]).astype(jnp.float32)
        return (jax.nn.sigmoid(logits) - labels).astype(jnp.bfloat16)

    def record(stores, visiting, anchor):
        weight_store, text_store = stores
        weights = compute_weights(visiting, anchor)
        place = anchor * row_count
        weight_store = lax.dynamic_update_slice_in_dim(weight_store, weights, place, 0)
        text_store = lax.dynamic_update_slice_in_dim(text_store, visiting, place, 0)
        return ((weight_store, text_store), weights)

    stores = (
        jnp.zeros((cycle_length * row_count, group_rows), jnp.bfloat16),
        jnp.zeros((cycle_length * row_count, feat_width), jnp.bfloat16),
    )
    stores, own_weights = record(stores, text_embeds, block_index)

    def step_one(turn_index, state):
        visiting, inner = state
        visiting = shifted(visiting, "blk", 1)
        inner, weights = record(inner, visiting, (block_index - turn_index) % cycle_length)
        return (visiting, inner)

    final_text, stores = lax.fori_loop(1, cycle_length, step_one, (text_embeds, stores))
    weight_part = stores[0]
    text_grads = lax.psum_scatter(
        LOGIT_SCALE * jnp.dot(weight_part, gathered, preferred_element_type=jnp.float32),
        "blk",
        scatter_dimension=0,
        tiled=True,
    )
    weight_store, text_store = stores
    weight_part = weight_store
    image_grads = lax.psum_scatter(
        (
            LOGIT_SCALE
            * lax.dot_general(
                weight_part,
                text_store,
                (((0,), (0,)), ((), ())),
                preferred_element_type=jnp.float32,
            )
        ).astype(jnp.bfloat16),
        "grp",
        scatter_dimension=0,
        tiled=True,
    ).astype(jnp.float32)
    return (image_grads, text_grads)


def solution(mesh):
    placed = (P(("blk", "grp"), None), P(("blk", "grp"), None))
    return jax.shard_map(
        local,
        mesh=mesh,
        in_specs=placed,
        out_specs=(P(("blk", "grp"), None), P(("blk", "grp"), None)),
        check_vma=False,
    )
```

profile of v0, /device:TPU:0, one launch (start us, length us, event | category | flops | bytes accessed | tf_op | source)
XLA Modules:
  0.0 95.5 jit_solution(1543377392238592608)
XLA Ops:
  8.0 0.0 copy-start
  8.0 0.0 all-reduce.3.cloned.1.call-start
  8.1 0.8 copy.22
  8.8 0.0 copy-done
  8.8 15.9 %all_gather.3 = bf16[128,1152]{1,0:T(8,128)(2,1)S(1)} all-gather(bf16[16,1152]{1,0:T(8,128)(2,1)S(1)} %copy-done), channel_id=1, replica_groups=mesh['blk'=4,'grp'=8] {'grp'}, dimensions={0}, use_global_device_ids=true | all-gather | bytes 331776 | tf_op jit(solution)/shard_map/all_gather | solution.py:19
  24.8 0.2 fusion.20
  25.0 15.5 %while.20 = (s32[]{:T(128)}, bf16[16,1152]{1,0:T(8,128)(2,1)S(1)}, bf16[64,128]{1,0:T(8,128)(2,1)S(1)}, bf16[64,1152]{1,0:T(8,128)(2,1)S(1)}, bf16[128,1152]{1,0...) while((s32[]{:T(128)}, bf16[16,1152]{1,0:T(8,128)(2,1)S(1)}, ...), condition=%wide.region_1.2_spmd.clone, body=%wide.region_0.1_spmd.clone.sunk | while | flops 4737189 | bytes 632784 | solution.py:58
  25.0 1.5 %collective-permute-start = (bf16[16,1152]{1,0:T(8,128)(2,1)S(1)}, bf16[16,1152]{1,0:T(8,128)(2,1)S(1)}, u32[]{:S(2)}, u32[]{:S(2)}) collective-permute-start(bf16[16,1152]{1,0:T(8,128)(2,1)S(1)} %get-tuple-element.327), channel_id=1, source_target_pairs={{0,8},{8,16},{16,24},{24,0},{1,9},{9,17},{17,25},{25,1},{2,10},{10... | collective-permute-start | bytes 110600 | tf_op jit(solution)/shard_map/while/body/eval_jaxpr/ppermute | solution.py:12
  26.6 3.4 %collective-permute-done = bf16[16,1152]{1,0:T(8,128)(2,1)S(1)} collective-permute-done((bf16[16,1152]{1,0:T(8,128)(2,1)S(1)}, bf16[16,1152]{1,0:T(8,128)(2,1)S(1)}, u32[]{:S(2)}, u32[]{:S(2)}) %collective-permute-start) | collective-permute-done | bytes 36896 | tf_op jit(solution)/shard_map/while/body/eval_jaxpr/ppermute | solution.py:12
  30.0 0.2 fusion.34
  30.2 0.6 collective-permute-start
  30.9 4.3 %collective-permute-done = bf16[16,1152]{1,0:T(8,128)(2,1)S(1)} collective-permute-done((bf16[16,1152]{1,0:T(8,128)(2,1)S(1)}, bf16[16,1152]{1,0:T(8,128)(2,1)S(1)}, u32[]{:S(2)}, u32[]{:S(2)}) %collective-permute-start) | collective-permute-done | bytes 36896 | tf_op jit(solution)/shard_map/while/body/eval_jaxpr/ppermute | solution.py:12
  35.1 0.2 fusion.34
  35.4 0.1 collective-permute-start
  35.5 4.8 %collective-permute-done = bf16[16,1152]{1,0:T(8,128)(2,1)S(1)} collective-permute-done((bf16[16,1152]{1,0:T(8,128)(2,1)S(1)}, bf16[16,1152]{1,0:T(8,128)(2,1)S(1)}, u32[]{:S(2)}, u32[]{:S(2)}) %collective-permute-start) | collective-permute-done | bytes 36896 | tf_op jit(solution)/shard_map/while/body/eval_jaxpr/ppermute | solution.py:12
  40.3 0.2 fusion.34
  40.6 0.9 convolution_multiply_fusion.2
  41.5 0.0 all-reduce.3.cloned.1.call-update
  41.5 0.0 reduce-scatter.2.cloned.1.call-start
  41.5 1.0 %fusion.12 = bf16[128,1152]{1,0:T(8,128)(2,1)} fusion(bf16[64,128]{1,0:T(8,128)(2,1)S(1)} %get-tuple-element.224, bf16[64,1152]{1,0:T(8,128)(2,1)S(1)} %get-tuple-element.225), kind=kOutput, calls=%fused_computation.15 | convolution fusion | flops 19169280 | bytes 458752 | tf_op jit(solution)/shard_map/dot_general | solution.py:71
  42.5 0.0 reduce-scatter.2.cloned.1.call-update
  42.6 0.0 copy-start.1
  42.6 0.6 copy-done.1
  43.2 0.6 dynamic-slice
  44.5 40.7 %all-reduce.3.cloned.1.call-done = f32[64,1152]{1,0:T(8,128)} async-done(((f32[64,1152]{1,0:T(8,128)}), f32[64,1152]{1,0:T(8,128)}) %all-reduce.3.cloned.1.call-update) | async-done | bytes 294928
  85.1 1.5 %constant_dynamic-slice_fusion = f32[16,1152]{1,0:T(8,128)} fusion(f32[64,1152]{1,0:T(8,128)} %all-reduce.3.cloned.1.call-done, u32[]{:T(128)S(6)} %multiply.5), kind=kLoop, calls=%fused_computation.26 | loop fusion | bytes 147460
  86.7 0.0 reduce-scatter.2.cloned.1.call-done
  86.7 1.4 %convert_element_type.35 = f32[16,1152]{1,0:T(8,128)} convert(bf16[16,1152]{1,0:T(8,128)(2,1)} %reduce-scatter.2.cloned.1.call-done) | non-fusion elementwise | flops 18432 | bytes 110592 | tf_op jit(solution)/shard_map/convert_element_type | solution.py:81
  (17 shorter events, 0.1 us)
Async XLA Ops:
  8.0 0.8 copy-start
  8.0 77.1 %all-reduce.3.cloned.1.call-start = ((), (), s32[]{:S(2)}) async-start(), calls=%async_computation.2 | async-start | bytes 589824
  25.0 4.9 %collective-permute-start = (bf16[16,1152]{1,0:T(8,128)(2,1)S(1)}, bf16[16,1152]{1,0:T(8,128)(2,1)S(1)}, u32[]{:S(2)}, u32[]{:S(2)}) collective-permute-start(bf16[16,1152]{1,0:T(8,128)(2,1)S(1)} %get-tuple-element.327), channel_id=1, source_target_pairs={{0,8},{8,16},{16,24},{24,0},{1,9},{9,17},{17,25},{25,1},{2,10},{10... | collective-permute-start | bytes 110600 | tf_op jit(solution)/shard_map/while/body/eval_jaxpr/ppermute | solution.py:12
  30.2 4.9 %collective-permute-start = (bf16[16,1152]{1,0:T(8,128)(2,1)S(1)}, bf16[16,1152]{1,0:T(8,128)(2,1)S(1)}, u32[]{:S(2)}, u32[]{:S(2)}) collective-permute-start(bf16[16,1152]{1,0:T(8,128)(2,1)S(1)} %get-tuple-element.327), channel_id=1, source_target_pairs={{0,8},{8,16},{16,24},{24,0},{1,9},{9,17},{17,25},{25,1},{2,10},{10... | collective-permute-start | bytes 110600 | tf_op jit(solution)/shard_map/while/body/eval_jaxpr/ppermute | solution.py:12
  35.4 4.9 %collective-permute-start = (bf16[16,1152]{1,0:T(8,128)(2,1)S(1)}, bf16[16,1152]{1,0:T(8,128)(2,1)S(1)}, u32[]{:S(2)}, u32[]{:S(2)}) collective-permute-start(bf16[16,1152]{1,0:T(8,128)(2,1)S(1)} %get-tuple-element.327), channel_id=1, source_target_pairs={{0,8},{8,16},{16,24},{24,0},{1,9},{9,17},{17,25},{25,1},{2,10},{10... | collective-permute-start | bytes 110600 | tf_op jit(solution)/shard_map/while/body/eval_jaxpr/ppermute | solution.py:12
  41.5 45.2 %reduce-scatter.2.cloned.1.call-start = ((), (), s32[]{:S(2)}) async-start(), calls=%async_computation.1 | async-start | bytes 331776 | tf_op jit(solution)/shard_map/reduce_scatter | solution.py:68
  42.6 0.7 copy-start.1
Sparse Core Ops, SparseCore 0:
  41.6 43.4 all-reduce.2
Sparse Core Ops, SparseCore 1:
  44.2 30.5 reduce-scatter.1
where the time goes:
time: 95.8 us; the launch traced here: 95.5 us
  waiting for transfers between devices  53.1 us (55%)
  between operations  16.2 us (17%)
  blocking collectives  15.9 us (17%)
  local copies, waits for them, and re-layouts  3.61 us (4%)
  matrix products  2.81 us (3%)
  starting transfers between devices  2.33 us (2%)
  other arithmetic  1.43 us (1%)
    unnamed x3, waiting for transfers between devices  40.7 us
    all_gather x1, blocking collectives, local(): gathered = lax.all_gather(image_embeds, 'grp', axis=0, tiled=True)  15.9 us
    ppermute x3, waiting for transfers between devices, shifted(): lax.ppermute(array, axis, [(i, (i + by) % peers) for i in range(peers)])  12.4 us
    unnamed x7, local copies, waits for them, and re-layouts  3.53 us
    ppermute x3, starting transfers between devices, shifted(): lax.ppermute(array, axis, [(i, (i + by) % peers) for i in range(peers)])  2.25 us
  transfers between devices with their start and end apart: 5, of which 4 were waited for; matrix products, arithmetic and copies ran while one was open for 3% of the time, Pallas kernels for 0%

commit v1 on v0

v1 whole, which is shorter than its diff:
```python
import functools

import jax
import jax.numpy as jnp
from jax import lax
from jax.experimental import pallas as pl
from jax.experimental.pallas import tpu as pltpu
from jax.sharding import PartitionSpec as P

LOGIT_SCALE = 0.044
LOGIT_BIAS = -4.0
MESH = pl.DeviceIdType.MESH


def offsets(count, inner):
    return [(o, i) for o in range(count // inner) for i in range(inner)]


def moved(index, count, inner, step, sign):
    outer = lax.rem(index // inner + sign * step[0] + count // inner, count // inner)
    return outer * inner + lax.rem(index % inner + sign * step[1] + inner, inner)


def kernel(
    n_blk, n_grp, blk_inner, pair, rows, chunk,
    image_ref, text_ref, image_out, text_out,
    images, texts, image_send, text_send, image_got, text_got, text_sum, image_own,
    local_sem, gi_send, gi_recv, gt_send, gt_recv, si_send, si_recv, st_send, st_recv,
):
    blk, grp = lax.axis_index("blk"), lax.axis_index("grp")
    image_steps = [(b, c) for b in offsets(n_blk, blk_inner) for c in range(pair)]
    text_steps = list(range(n_grp // pair))

    def image_peer(step, sign):
        return (moved(blk, n_blk, blk_inner, step[0], sign), moved(grp, n_grp, pair, (0, step[1]), sign))

    def text_peer(step, sign):
        return (blk, moved(grp, n_grp, pair, (step, 0), sign))

    image_slots = range(1, len(image_steps))
    text_slots = range(1, len(text_steps))

    own_image = pltpu.make_async_copy(image_ref, images.at[pl.ds(0, rows)], local_sem.at[0])
    own_text = pltpu.make_async_copy(text_ref, texts.at[pl.ds(0, rows)], local_sem.at[1])
    own_text.start()
    own_image.start()

    barrier = pltpu.get_barrier_semaphore()
    for s in image_slots:
        pl.semaphore_signal(barrier, inc=1, device_id=image_peer(image_steps[s], 1), device_id_type=MESH)
    for s in text_slots:
        pl.semaphore_signal(barrier, inc=1, device_id=text_peer(text_steps[s], 1), device_id_type=MESH)
    own_text.wait()
    own_image.wait()
    pl.semaphore_wait(barrier, len(image_slots) + len(text_slots))

    def remote(src, dst, send, recv, slot, device):
        return pltpu.make_async_remote_copy(
            src_ref=src, dst_ref=dst, send_sem=send.at[slot], recv_sem=recv.at[slot],
            device_id=device, device_id_type=MESH,
        )

    def part(ref, slot):
        return ref.at[pl.ds(slot * rows, rows)]

    text_gather = [
        remote(part(texts, 0), part(texts, s), gt_send, gt_recv, s, text_peer(text_steps[s], 1))
        for s in text_slots
    ]
    image_gather = [
        remote(part(images, 0), part(images, s), gi_send, gi_recv, s, image_peer(image_steps[s], 1))
        for s in image_slots
    ]
    for copy in text_gather + image_gather:
        copy.start()
    for copy in text_gather + image_gather:
        copy.wait_recv()

    total = images.shape[0]

    def weights_of(begin, is_first):
        logits = LOGIT_SCALE * lax.dot_general(
            images[pl.ds(begin, chunk)], texts[...], (((1,), (1,)), ((), ())),
            preferred_element_type=jnp.float32,
        ) + LOGIT_BIAS
        row = lax.broadcasted_iota(jnp.int32, logits.shape, 0) + begin
        column = lax.broadcasted_iota(jnp.int32, logits.shape, 1)
        labels = jnp.where((row == column) & (row < rows), 1.0, 0.0)
        return (lax.logistic(logits) - labels).astype(jnp.bfloat16)

    def image_terms(weights):
        return LOGIT_SCALE * jnp.dot(weights, texts[...], preferred_element_type=jnp.float32)

    def text_terms(weights, begin):
        return LOGIT_SCALE * lax.dot_general(
            weights, images[pl.ds(begin, chunk)], (((0,), (0,)), ((), ())),
            preferred_element_type=jnp.float32,
        )

    image_scatter = [
        remote(part(image_send, s), image_got.at[s], si_send, si_recv, s, image_peer(image_steps[s], -1))
        for s in image_slots
    ]
    text_scatter = [
        remote(part(text_send, s), text_got.at[s], st_send, st_recv, s, text_peer(text_steps[s], -1))
        for s in text_slots
    ]

    weights = weights_of(0, True)
    terms = image_terms(weights)
    image_own[...] = terms[:rows]
    image_send[pl.ds(0, chunk)] = terms.astype(jnp.bfloat16)
    if total == chunk:
        for copy in image_scatter:
            copy.start()
        text_sum[...] = text_terms(weights, 0)
    else:
        text_sum[...] = text_terms(weights, 0)

        def later(at, carry):
            begin = pl.multiple_of(at * chunk, chunk)
            weights = weights_of(begin, False)
            image_send[pl.ds(begin, chunk)] = image_terms(weights).astype(jnp.bfloat16)
            text_sum[...] += text_terms(weights, begin)
            return carry

        lax.fori_loop(1, total // chunk, later, 0)
        for copy in image_scatter:
            copy.start()
    text_send[...] = text_sum[...].astype(jnp.bfloat16)
    for copy in text_scatter:
        copy.start()

    for copy in image_scatter:
        copy.wait_recv()
    grads = image_own[...]
    for s in image_slots:
        grads += image_got[s].astype(jnp.float32)
    image_out[...] = grads
    for copy in text_scatter:
        copy.wait_recv()
    grads = text_sum[pl.ds(0, rows)]
    for s in text_slots:
        grads += text_got[s].astype(jnp.float32)
    text_out[...] = grads
    for copy in text_gather + image_gather + image_scatter + text_scatter:
        copy.wait_send()


def local(n_blk, n_grp, image_embeds, text_embeds):
    rows, width = image_embeds.shape
    pair = 2 if n_grp % 2 == 0 else 1
    blk_inner = 2 if n_blk % 2 == 0 else 1
    n_image, n_text = n_blk * pair, n_grp // pair
    total = n_image * rows
    chunk = 128 if total % 128 == 0 else total
    bf16, f32 = jnp.bfloat16, jnp.float32
    out = jax.ShapeDtypeStruct((rows, width), f32)
    return pl.pallas_call(
        functools.partial(kernel, n_blk, n_grp, blk_inner, pair, rows, chunk),
        out_shape=(out, out),
        in_specs=[pl.BlockSpec(memory_space=pl.ANY)] * 2,
        out_specs=[pl.BlockSpec(memory_space=pltpu.VMEM)] * 2,
        scratch_shapes=[
            pltpu.VMEM((total, width), bf16),
            pltpu.VMEM((n_text * rows, width), bf16),
            pltpu.VMEM((total, width), bf16),
            pltpu.VMEM((n_text * rows, width), bf16),
            pltpu.VMEM((n_image, rows, width), bf16),
            pltpu.VMEM((n_text, rows, width), bf16),
            pltpu.VMEM((n_text * rows, width), f32),
            pltpu.VMEM((rows, width), f32),
            pltpu.SemaphoreType.DMA((2,)),
            *[pltpu.SemaphoreType.DMA((n,)) for n in (n_image, n_image, n_text, n_text) * 2],
        ],
        compiler_params=pltpu.CompilerParams(
            collective_id=0, has_side_effects=True, vmem_limit_bytes=40 * 1024 * 1024
        ),
    )(image_embeds, text_embeds)


def solution(mesh):
    placed = (P(("blk", "grp"), None), P(("blk", "grp"), None))
    return jax.shard_map(
        functools.partial(local, mesh.shape["blk"], mesh.shape["grp"]),
        mesh=mesh,
        in_specs=placed,
        out_specs=placed,
        check_vma=False,
    )
```

time: 95.8 us -> 20.5 us (0.21)
  waiting for transfers between devices: 53.1 us -> 0 us
  Pallas kernels: 0 us -> 16.9 us
  blocking collectives: 15.9 us -> 0 us
  between operations: 16.2 us -> 0.65 us
  matrix products: 2.81 us -> 0 us
  starting transfers between devices: 2.33 us -> 0 us
  other arithmetic: 1.43 us -> 0 us
    unnamed x3 -> x0, waiting for transfers between devices: 40.7 us -> none
    pallas_call x0 -> x1, Pallas kernels: none -> 16.9 us  [local(): pl.pallas_call(functools.partial(kernel, n_blk, n_grp, blk_inner, pair, r...]
    all_gather x1 -> x0, blocking collectives: 15.9 us -> none  [local(): gathered = lax.all_gather(image_embeds, 'grp', axis=0, tiled=True)]
    ppermute x3 -> x0, waiting for transfers between devices: 12.4 us -> none  [shifted(): lax.ppermute(array, axis, [(i, (i + by) % peers) for i in range(peers)])]
    dot_general x6 -> x0, matrix products: 2.81 us -> none  [the longest x1 0.99 us: local(): lax.dot_general(weight_part, text_store, (((0,), (0,)), ((), ())), prefer...]
    ppermute x3 -> x0, starting transfers between devices: 2.25 us -> none  [shifted(): lax.ppermute(array, axis, [(i, (i + by) % peers) for i in range(peers)])]
    convert_element_type x1 -> x0, other arithmetic: 1.41 us -> none  [local(): image_grads = lax.psum_scatter((LOGIT_SCALE * lax.dot_general(weight_part...]
    unnamed x7 -> x6, local copies, waits for them, and re-layouts: 3.53 us -> 2.8 us
  transfers between devices with their start and end apart: 5 -> 0, of which waited for: 4 -> 0; matrix products, arithmetic and copies ran while one was open for 3% -> 0% of each run, Pallas kernels for 0% -> 0%
where the time goes in v1:
time: 20.5 us; the launch traced here: 20.3 us
  Pallas kernels  16.9 us (82%)
  local copies, waits for them, and re-layouts  2.8 us (14%)
  between operations  0.65 us (3%)
    pallas_call x1, Pallas kernels, local(): pl.pallas_call(functools.partial(kernel, n_blk, n_grp, blk_inner, pair, r...  16.9 us
    unnamed x6, local copies, waits for them, and re-layouts  2.8 us

profile of v1, /device:TPU:0, one launch (start us, length us, event | category | flops | bytes accessed | tf_op | source)
XLA Modules:
  0.0 20.3 jit_solution(1344353527255001737)
XLA Ops:
  0.6 0.0 copy-start
  0.6 0.8 %copy-done = bf16[16,1152]{1,0:T(8,128)(2,1)S(1)} copy-done((bf16[16,1152]{1,0:T(8,128)(2,1)S(1)}, bf16[16,1152]{1,0:T(8,128)(2,1)}, u32[]{:S(2)}) %copy-start) | copy-done | bytes 36888
  1.4 0.0 copy-start.1
  1.4 0.8 %copy-done.1 = bf16[16,1152]{1,0:T(8,128)(2,1)S(1)} copy-done((bf16[16,1152]{1,0:T(8,128)(2,1)S(1)}, bf16[16,1152]{1,0:T(8,128)(2,1)}, u32[]{:S(2)}) %copy-start.1) | copy-done | bytes 36888
  2.2 16.9 %shard_map.41 = (f32[16,1152]{1,0:T(8,128)S(1)}, f32[16,1152]{1,0:T(8,128)S(1)}) custom-call(bf16[16,1152]{1,0:T(8,128)(2,1)S(1)} %copy-done, bf16[16,1152]{1,0:T(8,128)(2,1)S(1)} %copy-done.1), custom_call_target="tpu_custom_call" | custom-call | tf_op jit(solution)/shard_map/pallas_call | solution.py:159
  19.0 0.6 %copy.6 = f32[16,1152]{1,0:T(8,128)} copy(f32[16,1152]{1,0:T(8,128)S(1)} %get-tuple-element.4) | data formatting | bytes 147456
  19.7 0.6 %copy.7 = f32[16,1152]{1,0:T(8,128)} copy(f32[16,1152]{1,0:T(8,128)S(1)} %get-tuple-element.5) | data formatting | bytes 147456
Async XLA Ops:
  0.6 0.8 %copy-start = (bf16[16,1152]{1,0:T(8,128)(2,1)S(1)}, bf16[16,1152]{1,0:T(8,128)(2,1)}, u32[]{:S(2)}) copy-start(bf16[16,1152]{1,0:T(8,128)(2,1)} %image_ref.1) | copy-start | bytes 110596
  1.4 0.8 %copy-start.1 = (bf16[16,1152]{1,0:T(8,128)(2,1)S(1)}, bf16[16,1152]{1,0:T(8,128)(2,1)}, u32[]{:S(2)}) copy-start(bf16[16,1152]{1,0:T(8,128)(2,1)} %text_ref.1) | copy-start | bytes 110596

commit v2 on v1

--- a/solution.py
+++ b/solution.py
@@ -9,6 +9,8 @@
 
 LOGIT_SCALE = 0.044
 LOGIT_BIAS = -4.0
+SPLIT = 1
+TEXT_FIRST = True
 MESH = pl.DeviceIdType.MESH
 
 
@@ -23,7 +25,7 @@
 
 def kernel(
     n_blk, n_grp, blk_inner, pair, rows, chunk,
-    image_ref, text_ref, image_out, text_out,
+    image_ref, text_ref, outs,
     images, texts, image_send, text_send, image_got, text_got, text_sum, image_own,
     local_sem, gi_send, gi_recv, gt_send, gt_recv, si_send, si_recv, st_send, st_recv,
 ):
@@ -42,16 +44,12 @@
 
     own_image = pltpu.make_async_copy(image_ref, images.at[pl.ds(0, rows)], local_sem.at[0])
     own_text = pltpu.make_async_copy(text_ref, texts.at[pl.ds(0, rows)], local_sem.at[1])
-    own_text.start()
-    own_image.start()
 
     barrier = pltpu.get_barrier_semaphore()
     for s in image_slots:
         pl.semaphore_signal(barrier, inc=1, device_id=image_peer(image_steps[s], 1), device_id_type=MESH)
     for s in text_slots:
         pl.semaphore_signal(barrier, inc=1, device_id=text_peer(text_steps[s], 1), device_id_type=MESH)
-    own_text.wait()
-    own_image.wait()
     pl.semaphore_wait(barrier, len(image_slots) + len(text_slots))
 
     def remote(src, dst, send, recv, slot, device):
@@ -64,21 +62,20 @@
         return ref.at[pl.ds(slot * rows, rows)]
 
     text_gather = [
-        remote(part(texts, 0), part(texts, s), gt_send, gt_recv, s, text_peer(text_steps[s], 1))
+        remote(text_ref, part(texts, s), gt_send, gt_recv, s, text_peer(text_steps[s], 1))
         for s in text_slots
     ]
     image_gather = [
-        remote(part(images, 0), part(images, s), gi_send, gi_recv, s, image_peer(image_steps[s], 1))
+        remote(image_ref, part(images, s), gi_send, gi_recv, s, image_peer(image_steps[s], 1))
         for s in image_slots
     ]
     for copy in text_gather + image_gather:
         copy.start()
-    for copy in text_gather + image_gather:
-        copy.wait_recv()
-
+    own_text.start()
+    own_image.start()
     total = images.shape[0]
 
-    def weights_of(begin, is_first):
+    def weights_of(begin):
         logits = LOGIT_SCALE * lax.dot_general(
             images[pl.ds(begin, chunk)], texts[...], (((1,), (1,)), ((), ())),
             preferred_element_type=jnp.float32,
@@ -91,9 +88,9 @@
     def image_terms(weights):
         return LOGIT_SCALE * jnp.dot(weights, texts[...], preferred_element_type=jnp.float32)
 
-    def text_terms(weights, begin):
+    def text_terms(weights, begin, count):
         return LOGIT_SCALE * lax.dot_general(
-            weights, images[pl.ds(begin, chunk)], (((0,), (0,)), ((), ())),
+            weights, images[pl.ds(begin, count)], (((0,), (0,)), ((), ())),
             preferred_element_type=jnp.float32,
         )
 
@@ -106,43 +103,72 @@
         for s in text_slots
     ]
 
-    weights = weights_of(0, True)
-    terms = image_terms(weights)
-    image_own[...] = terms[:rows]
-    image_send[pl.ds(0, chunk)] = terms.astype(jnp.bfloat16)
-    if total == chunk:
+    def arrived(begin):
+        for copy in image_gather[max(begin // rows - 1, 0):(begin + chunk) // rows - 1]:
+            copy.wait_recv()
+
+    own_text.wait()
+    own_image.wait()
+    for copy in text_gather:
+        copy.wait_recv()
+    if total <= 256:
+        parts = []
+        for begin in range(0, total, chunk):
+            arrived(begin)
+            parts.append(weights_of(begin))
+            if TEXT_FIRST and begin + chunk == total:
+                text_sum[...] = text_terms(jnp.concatenate(parts), 0, total)
+                text_send[...] = text_sum[...].astype(jnp.bfloat16)
+                for copy in text_scatter:
+                    copy.start()
+            terms = image_terms(parts[-1])
+            if begin == 0:
+                image_own[...] = terms[:rows]
+            image_send[pl.ds(begin, chunk)] = terms.astype(jnp.bfloat16)
+            for copy in image_scatter[max(begin // rows - 1, 0):(begin + chunk) // rows - 1]:
+                copy.start()
+        if not TEXT_FIRST:
+            text_sum[...] = text_terms(jnp.concatenate(parts), 0, total)
+            text_send[...] = text_sum[...].astype(jnp.bfloat16)
+            for copy in text_scatter:
+                copy.start()
+    else:
+        for copy in image_gather:
+            copy.wait_recv()
+        text_sum[...] = jnp.zeros_like(text_sum)
+
+        def step(at, carry):
+            begin = pl.multiple_of(at * chunk, chunk)
+            weights = weights_of(begin)
+            terms = image_terms(weights)
+
+            @pl.when(at == 0)
+            def _():
+                image_own[...] = terms[:rows]
+
+            image_send[pl.ds(begin, chunk)] = terms.astype(jnp.bfloat16)
+            text_sum[...] += text_terms(weights, begin, chunk)
+            return carry
+
+        lax.fori_loop(0, total // chunk, step, 0)
         for copy in image_scatter:
             copy.start()
-        text_sum[...] = text_terms(weights, 0)
-    else:
-        text_sum[...] = text_terms(weights, 0)
-
-        def later(at, carry):
-            begin = pl.multiple_of(at * chunk, chunk)
-            weights = weights_of(begin, False)
-            image_send[pl.ds(begin, chunk)] = image_terms(weights).astype(jnp.bfloat16)
-            text_sum[...] += text_terms(weights, begin)
-            return carry
-
-        lax.fori_loop(1, total // chunk, later, 0)
-        for copy in image_scatter:
+        text_send[...] = text_sum[...].astype(jnp.bfloat16)
+        for copy in text_scatter:
             copy.start()
-    text_send[...] = text_sum[...].astype(jnp.bfloat16)
-    for copy in text_scatter:
-        copy.start()
 
     for copy in image_scatter:
         copy.wait_recv()
     grads = image_own[...]
     for s in image_slots:
         grads += image_got[s].astype(jnp.float32)
-    image_out[...] = grads
+    outs[0] = grads
     for copy in text_scatter:
         copy.wait_recv()
     grads = text_sum[pl.ds(0, rows)]
     for s in text_slots:
         grads += text_got[s].astype(jnp.float32)
-    text_out[...] = grads
+    outs[1] = grads
     for copy in text_gather + image_gather + image_scatter + text_scatter:
         copy.wait_send()
 
@@ -153,14 +179,14 @@
     blk_inner = 2 if n_blk % 2 == 0 else 1
     n_image, n_text = n_blk * pair, n_grp // pair
     total = n_image * rows
-    chunk = 128 if total % 128 == 0 else total
+    chunk = total // SPLIT if total <= 256 else 128
     bf16, f32 = jnp.bfloat16, jnp.float32
     out = jax.ShapeDtypeStruct((rows, width), f32)
-    return pl.pallas_call(
+    sums = pl.pallas_call(
         functools.partial(kernel, n_blk, n_grp, blk_inner, pair, rows, chunk),
-        out_shape=(out, out),
+        out_shape=jax.ShapeDtypeStruct((2, rows, width), f32),
         in_specs=[pl.BlockSpec(memory_space=pl.ANY)] * 2,
-        out_specs=[pl.BlockSpec(memory_space=pltpu.VMEM)] * 2,
+        out_specs=pl.BlockSpec(memory_space=pltpu.VMEM),
         scratch_shapes=[
             pltpu.VMEM((total, width), bf16),
             pltpu.VMEM((n_text * rows, width), bf16),
@@ -177,6 +203,7 @@
             collective_id=0, has_side_effects=True, vmem_limit_bytes=40 * 1024 * 1024
         ),
     )(image_embeds, text_embeds)
+    return sums[0], sums[1]
 
 
 def solution(mesh):

time: 20.5 us -> 19.6 us (0.956)
  local copies, waits for them, and re-layouts: 2.8 us -> 2.19 us
  Pallas kernels: 16.9 us -> 16.5 us
    unnamed x6 -> x4, local copies, waits for them, and re-layouts: 2.8 us -> 1.53 us
    squeeze x0 -> x1, local copies, waits for them, and re-layouts: none -> 0.66 us  [local(): return (sums[0], sums[1])]
    pallas_call x1, Pallas kernels: 16.9 us -> 16.5 us  [local(): pl.pallas_call(functools.partial(kernel, n_blk, n_grp, blk_inner, pair, r...]
where the time goes in v2:
time: 19.6 us; the launch traced here: 19.3 us
  Pallas kernels  16.5 us (84%)
  local copies, waits for them, and re-layouts  2.19 us (11%)
  between operations  0.65 us (3%)
    pallas_call x1, Pallas kernels, local(): pl.pallas_call(functools.partial(kernel, n_blk, n_grp, blk_inner, pair, r...  16.5 us
    unnamed x4, local copies, waits for them, and re-layouts  1.53 us
    squeeze x1, local copies, waits for them, and re-layouts, local(): return (sums[0], sums[1])  0.66 us

profile of v2, /device:TPU:0, one launch (start us, length us, event | category | flops | bytes accessed | tf_op | source)
XLA Modules:
  0.0 19.3 jit_solution(18045320080514094967)
XLA Ops:
  0.6 0.0 copy-start
  0.6 0.8 %copy-done = bf16[16,1152]{1,0:T(8,128)(2,1)S(1)} copy-done((bf16[16,1152]{1,0:T(8,128)(2,1)S(1)}, bf16[16,1152]{1,0:T(8,128)(2,1)}, u32[]{:S(2)}) %copy-start) | copy-done | bytes 36888
  1.4 0.0 copy-start.1
  1.4 0.8 %copy-done.1 = bf16[16,1152]{1,0:T(8,128)(2,1)S(1)} copy-done((bf16[16,1152]{1,0:T(8,128)(2,1)S(1)}, bf16[16,1152]{1,0:T(8,128)(2,1)}, u32[]{:S(2)}) %copy-start.1) | copy-done | bytes 36888
  2.2 16.5 %shard_map.41 = f32[2,16,1152]{2,1,0:T(8,128)S(1)} custom-call(bf16[16,1152]{1,0:T(8,128)(2,1)S(1)} %copy-done, bf16[16,1152]{1,0:T(8,128)(2,1)S(1)} %copy-done.1), custom_call_target="tpu_custom_call" | custom-call | tf_op jit(solution)/shard_map/pallas_call | solution.py:185
  18.6 0.7 %slice_bitcast_fusion = (f32[16,1152]{1,0:T(8,128)}, f32[16,1152]{1,0:T(8,128)}) fusion(f32[2,16,1152]{2,1,0:T(8,128)S(1)} %shard_map.41), kind=kLoop, calls=%fused_computation | loop fusion | bytes 294912 | tf_op jit(solution)/shard_map/squeeze | solution.py:206
Async XLA Ops:
  0.6 0.8 %copy-start = (bf16[16,1152]{1,0:T(8,128)(2,1)S(1)}, bf16[16,1152]{1,0:T(8,128)(2,1)}, u32[]{:S(2)}) copy-start(bf16[16,1152]{1,0:T(8,128)(2,1)} %image_ref.1) | copy-start | bytes 110596
  1.4 0.8 %copy-start.1 = (bf16[16,1152]{1,0:T(8,128)(2,1)S(1)}, bf16[16,1152]{1,0:T(8,128)(2,1)}, u32[]{:S(2)}) copy-start(bf16[16,1152]{1,0:T(8,128)(2,1)} %text_ref.1) | copy-start | bytes 110596

commit v3 on v2

--- a/solution.py
+++ b/solution.py
@@ -46,10 +46,10 @@
     own_text = pltpu.make_async_copy(text_ref, texts.at[pl.ds(0, rows)], local_sem.at[1])
 
     barrier = pltpu.get_barrier_semaphore()
-    for s in image_slots:
+    for s in text_slots[::-1]:
+        pl.semaphore_signal(barrier, inc=1, device_id=text_peer(text_steps[s], 1), device_id_type=MESH)
+    for s in image_slots[::-1]:
         pl.semaphore_signal(barrier, inc=1, device_id=image_peer(image_steps[s], 1), device_id_type=MESH)
-    for s in text_slots:
-        pl.semaphore_signal(barrier, inc=1, device_id=text_peer(text_steps[s], 1), device_id_type=MESH)
     pl.semaphore_wait(barrier, len(image_slots) + len(text_slots))
 
     def remote(src, dst, send, recv, slot, device):
@@ -69,7 +69,8 @@
         remote(image_ref, part(images, s), gi_send, gi_recv, s, image_peer(image_steps[s], 1))
         for s in image_slots
     ]
-    for copy in text_gather + image_gather:
+    order = image_gather[2::2] + text_gather[::-1] + image_gather[1::2] + image_gather[:1]
+    for copy in order:
         copy.start()
     own_text.start()
     own_image.start()
@@ -125,7 +126,8 @@
             if begin == 0:
                 image_own[...] = terms[:rows]
             image_send[pl.ds(begin, chunk)] = terms.astype(jnp.bfloat16)
-            for copy in image_scatter[max(begin // rows - 1, 0):(begin + chunk) // rows - 1]:
+            sends = image_scatter[max(begin // rows - 1, 0):(begin + chunk) // rows - 1]
+            for copy in sends[2::2] + sends[1::2] + sends[:1]:
                 copy.start()
         if not TEXT_FIRST:
             text_sum[...] = text_terms(jnp.concatenate(parts), 0, total)
@@ -157,6 +159,8 @@
         for copy in text_scatter:
             copy.start()
 
+    for copy in text_gather + image_gather + image_scatter + text_scatter:
+        copy.wait_send()
     for copy in image_scatter:
         copy.wait_recv()
     grads = image_own[...]
@@ -169,8 +173,6 @@
     for s in text_slots:
         grads += text_got[s].astype(jnp.float32)
     outs[1] = grads
-    for copy in text_gather + image_gather + image_scatter + text_scatter:
-        copy.wait_send()
 
 
 def local(n_blk, n_grp, image_embeds, text_embeds):

time: 19.6 us -> 19.4 us (0.990)
  Pallas kernels: 16.5 us -> 16.3 us
where the time goes in v3:
time: 19.4 us; the launch traced here: 19.1 us
  Pallas kernels  16.3 us (84%)
  local copies, waits for them, and re-layouts  2.19 us (11%)
  between operations  0.65 us (3%)
    pallas_call x1, Pallas kernels, local(): pl.pallas_call(functools.partial(kernel, n_blk, n_grp, blk_inner, pair, r...  16.3 us
    unnamed x4, local copies, waits for them, and re-layouts  1.53 us
    squeeze x1, local copies, waits for them, and re-layouts, local(): return (sums[0], sums[1])  0.66 us

profile of v3, /device:TPU:0, one launch (start us, length us, event | category | flops | bytes accessed | tf_op | source)
XLA Modules:
  0.0 19.1 jit_solution(5510959549179124732)
XLA Ops:
  0.6 0.0 copy-start
  0.6 0.8 %copy-done = bf16[16,1152]{1,0:T(8,128)(2,1)S(1)} copy-done((bf16[16,1152]{1,0:T(8,128)(2,1)S(1)}, bf16[16,1152]{1,0:T(8,128)(2,1)}, u32[]{:S(2)}) %copy-start) | copy-done | bytes 36888
  1.4 0.0 copy-start.1
  1.4 0.8 %copy-done.1 = bf16[16,1152]{1,0:T(8,128)(2,1)S(1)} copy-done((bf16[16,1152]{1,0:T(8,128)(2,1)S(1)}, bf16[16,1152]{1,0:T(8,128)(2,1)}, u32[]{:S(2)}) %copy-start.1) | copy-done | bytes 36888
  2.2 16.3 %shard_map.41 = f32[2,16,1152]{2,1,0:T(8,128)S(1)} custom-call(bf16[16,1152]{1,0:T(8,128)(2,1)S(1)} %copy-done, bf16[16,1152]{1,0:T(8,128)(2,1)S(1)} %copy-done.1), custom_call_target="tpu_custom_call" | custom-call | tf_op jit(solution)/shard_map/pallas_call | solution.py:187
  18.5 0.7 %slice_bitcast_fusion = (f32[16,1152]{1,0:T(8,128)}, f32[16,1152]{1,0:T(8,128)}) fusion(f32[2,16,1152]{2,1,0:T(8,128)S(1)} %shard_map.41), kind=kLoop, calls=%fused_computation | loop fusion | bytes 294912 | tf_op jit(solution)/shard_map/squeeze | solution.py:208
Async XLA Ops:
  0.6 0.8 %copy-start = (bf16[16,1152]{1,0:T(8,128)(2,1)S(1)}, bf16[16,1152]{1,0:T(8,128)(2,1)}, u32[]{:S(2)}) copy-start(bf16[16,1152]{1,0:T(8,128)(2,1)} %image_ref.1) | copy-start | bytes 110596
  1.4 0.8 %copy-start.1 = (bf16[16,1152]{1,0:T(8,128)(2,1)S(1)}, bf16[16,1152]{1,0:T(8,128)(2,1)}, u32[]{:S(2)}) copy-start(bf16[16,1152]{1,0:T(8,128)(2,1)} %text_ref.1) | copy-start | bytes 110596

commit v4 on v3

--- a/solution.py
+++ b/solution.py
@@ -120,7 +120,7 @@
             if TEXT_FIRST and begin + chunk == total:
                 text_sum[...] = text_terms(jnp.concatenate(parts), 0, total)
                 text_send[...] = text_sum[...].astype(jnp.bfloat16)
-                for copy in text_scatter:
+                for copy in text_scatter[::-1]:
                     copy.start()
             terms = image_terms(parts[-1])
             if begin == 0:
@@ -161,16 +161,14 @@
 
     for copy in text_gather + image_gather + image_scatter + text_scatter:
         copy.wait_send()
-    for copy in image_scatter:
-        copy.wait_recv()
     grads = image_own[...]
     for s in image_slots:
+        image_scatter[s - 1].wait_recv()
         grads += image_got[s].astype(jnp.float32)
     outs[0] = grads
-    for copy in text_scatter:
-        copy.wait_recv()
     grads = text_sum[pl.ds(0, rows)]
     for s in text_slots:
+        text_scatter[s - 1].wait_recv()
         grads += text_got[s].astype(jnp.float32)
     outs[1] = grads
 

time: 19.4 us -> 19.2 us (0.990)
  Pallas kernels: 16.3 us -> 16.1 us
where the time goes in v4:
time: 19.2 us; the launch traced here: 19 us
  Pallas kernels  16.1 us (84%)
  local copies, waits for them, and re-layouts  2.19 us (11%)
  between operations  0.65 us (3%)
    pallas_call x1, Pallas kernels, local(): pl.pallas_call(functools.partial(kernel, n_blk, n_grp, blk_inner, pair, r...  16.1 us
    unnamed x4, local copies, waits for them, and re-layouts  1.53 us
    squeeze x1, local copies, waits for them, and re-layouts, local(): return (sums[0], sums[1])  0.66 us

profile of v4, /device:TPU:0, one launch (start us, length us, event | category | flops | bytes accessed | tf_op | source)
XLA Modules:
  0.0 19.0 jit_solution(7810129033796909194)
XLA Ops:
  0.6 0.0 copy-start
  0.6 0.8 %copy-done = bf16[16,1152]{1,0:T(8,128)(2,1)S(1)} copy-done((bf16[16,1152]{1,0:T(8,128)(2,1)S(1)}, bf16[16,1152]{1,0:T(8,128)(2,1)}, u32[]{:S(2)}) %copy-start) | copy-done | bytes 36888
  1.4 0.0 copy-start.1
  1.4 0.8 %copy-done.1 = bf16[16,1152]{1,0:T(8,128)(2,1)S(1)} copy-done((bf16[16,1152]{1,0:T(8,128)(2,1)S(1)}, bf16[16,1152]{1,0:T(8,128)(2,1)}, u32[]{:S(2)}) %copy-start.1) | copy-done | bytes 36888
  2.2 16.1 %shard_map.41 = f32[2,16,1152]{2,1,0:T(8,128)S(1)} custom-call(bf16[16,1152]{1,0:T(8,128)(2,1)S(1)} %copy-done, bf16[16,1152]{1,0:T(8,128)(2,1)S(1)} %copy-done.1), custom_call_target="tpu_custom_call" | custom-call | tf_op jit(solution)/shard_map/pallas_call | solution.py:185
  18.3 0.7 %slice_bitcast_fusion = (f32[16,1152]{1,0:T(8,128)}, f32[16,1152]{1,0:T(8,128)}) fusion(f32[2,16,1152]{2,1,0:T(8,128)S(1)} %shard_map.41), kind=kLoop, calls=%fused_computation | loop fusion | bytes 294912 | tf_op jit(solution)/shard_map/squeeze | solution.py:206
Async XLA Ops:
  0.6 0.8 %copy-start = (bf16[16,1152]{1,0:T(8,128)(2,1)S(1)}, bf16[16,1152]{1,0:T(8,128)(2,1)}, u32[]{:S(2)}) copy-start(bf16[16,1152]{1,0:T(8,128)(2,1)} %image_ref.1) | copy-start | bytes 110596
  1.4 0.8 %copy-start.1 = (bf16[16,1152]{1,0:T(8,128)(2,1)S(1)}, bf16[16,1152]{1,0:T(8,128)(2,1)}, u32[]{:S(2)}) copy-start(bf16[16,1152]{1,0:T(8,128)(2,1)} %text_ref.1) | copy-start | bytes 110596
